TPU v7x, 512 devices: a whole 4x4x16 slice. The times are simulated.
512 devices in a mesh: dp: 8 (over x, y_lo), fsdp: 64 (over y_hi, z, core).
Axes of the slice: x: 4, y: 4 (y_hi: 2, y_lo: 2; y = y_hi * 2 + y_lo), z: 16, core: 2. Of those that a mesh axis runs over, the one named last changes fastest.
Arguments:
- tokens: bfloat16 [3072, 4096], P(('dp', 'fsdp')), may hold values from -24 to 24
- w_gate: bfloat16 [4096, 16384], P('dp', 'fsdp'), may hold values from -0.09375 to 0.09375
- w_up: bfloat16 [4096, 16384], P('dp', 'fsdp'), may hold values from -0.09375 to 0.09375
- probe_gate: bfloat16 [4096, 16384], P('dp', 'fsdp'), may hold values from -0.09375 to 0.09375
- probe_up: bfloat16 [4096, 16384], P('dp', 'fsdp'), may hold values from -0.09375 to 0.09375
- w_down: bfloat16 [16384, 4096], P('fsdp', 'dp'), may hold values from -0.09375 to 0.09375
- out_grad: bfloat16 [3072, 4096], P(('dp', 'fsdp')), may hold values from -6 to 6
Outputs:
- hvp_gate: float32 [4096, 16384], P('dp', 'fsdp')
- hvp_up: float32 [4096, 16384], P('dp', 'fsdp')
All inputs are finite; a program needn't handle non-finite values.
Results may differ from a plain program's by a relative error of at most 0.015.
Values may be sent and summed in bfloat16 or wider, within the bound.
A program may use at most 64 MiB of HBM per device.

v0:
```python
import jax
import jax.numpy as jnp
from jax import lax
from jax.sharding import PartitionSpec as P


def normalize(tokens):
    values = tokens.astype(jnp.float32)
    return (values * lax.rsqrt(jnp.mean(values * values, axis=1, keepdims=True) + 1e-05)).astype(
        jnp.bfloat16
    )


def per_device(tokens, w_gate, w_up, probe_gate, probe_up, w_down, out_grad):
    local = normalize(tokens)
    normed, grads = (
        lax.all_gather(local, "fsdp", axis=0, tiled=True),
        lax.all_gather(out_grad, "fsdp", axis=0, tiled=True),
    )
    rows = normed.shape[0]
    width = w_gate.shape[1]
    groups = lax.axis_size("dp")
    scale = 1.0 / float(rows * groups) ** 0.5

    def add_rows(piece):
        return jnp.dot(normed, piece, preferred_element_type=jnp.float32)

    def add_two(pieces):
        return (add_rows(pieces[0]), add_rows(pieces[1]))

    gate, up = add_two(
        (
            lax.all_gather(w_gate, "dp", axis=0, tiled=True),
            lax.all_gather(w_up, "dp", axis=0, tiled=True),
        )
    )
    tgate, tup = add_two(
        (
            lax.all_gather(probe_gate, "dp", axis=0, tiled=True),
            lax.all_gather(probe_up, "dp", axis=0, tiled=True),
        )
    )
    dhid = (
        lax.dot_general(
            grads,
            lax.all_gather(w_down, "dp", axis=1, tiled=True),
            (((1,), (1,)), ((), ())),
            preferred_element_type=jnp.float32,
        )
        * scale
    )
    sig = jax.nn.sigmoid(gate)
    first = sig * (1.0 + gate * (1.0 - sig))
    second = sig * (1.0 - sig) * (2.0 + gate * (1.0 - 2.0 * sig))
    left = (dhid * (tup * first + up * second * tgate)).astype(jnp.bfloat16)
    right = (dhid * first * tgate).astype(jnp.bfloat16)
    joined = jnp.concatenate([left, right], axis=1)
    model_width = tokens.shape[1]
    owned = model_width // groups
    full = lax.dot_general(
        normed, joined, (((0,), (0,)), ((), ())), preferred_element_type=jnp.float32
    )
    summed = lax.psum(full.astype(jnp.bfloat16), "dp").astype(jnp.float32)
    mine = lax.dynamic_slice_in_dim(summed, lax.axis_index("dp") * owned, owned, 0)
    return (mine[:, :width], mine[:, width:])


def solution(mesh):
    placed = (
        P(("dp", "fsdp"), None),
        P("dp", "fsdp"),
        P("dp", "fsdp"),
        P("dp", "fsdp"),
        P("dp", "fsdp"),
        P("fsdp", "dp"),
        P(("dp", "fsdp"), None),
    )
    return jax.shard_map(
        per_device,
        mesh=mesh,
        in_specs=placed,
        out_specs=(P("dp", "fsdp"), P("dp", "fsdp")),
        check_vma=False,
    )
```

profile of v0, /device:TPU:4, one launch (start us, length us, event | category | flops | bytes accessed | tf_op | source)
XLA Modules:
  0.0 831.8 jit_solution(11654940961844968792)
XLA Ops:
  7.2 1.0 fusion.10
  8.2 1.6 fusion.12
  9.8 0.7 all-gather.22.cloned.1.call-update
  10.6 0.7 all-gather.14.cloned.1.call-update
  11.9 0.5 all-gather.18.cloned.1.call-update
  13.1 0.7 all-gather.12.cloned.1.call-update
  13.8 153.6 %all-gather.20.cloned.1.call-done = bf16[64,6,4096]{2,1,0:T(8,128)(2,1)} async-done(((bf16[1,6,4096]{2,1,0:T(8,128)(2,1)}), bf16[64,6,4096]{2,1,0:T(8,128)(2,1)}) %all-gather.20.cloned.1.call-update) | async-done | bytes 3145744 | tf_op jit(solution)/shard_map/all_gather | solution.py:17
  167.4 4.2 reshape.13
  171.5 144.6 %all-gather.22.cloned.1.call-done = bf16[64,6,4096]{2,1,0:T(8,128)(2,1)} async-done(((bf16[1,6,4096]{2,1,0:T(8,128)(2,1)}), bf16[64,6,4096]{2,1,0:T(8,128)(2,1)}) %all-gather.22.cloned.1.call-update) | async-done | bytes 3145744 | tf_op jit(solution)/shard_map/all_gather | solution.py:18
  316.2 5.7 reshape.15
  321.9 49.7 %all-gather.14.cloned.1.call-done = bf16[4096,256]{1,0:T(8,128)(2,1)} async-done(((bf16[512,256]{1,0:T(8,128)(2,1)}), bf16[4096,256]{1,0:T(8,128)(2,1)}) %all-gather.14.cloned.1.call-update) | async-done | bytes 2097168 | tf_op jit(solution)/shard_map/all_gather | solution.py:33
  371.6 3.6 fusion.15
  375.2 57.5 %all-gather.10.cloned.1.call-done = bf16[256,4096]{1,0:T(8,128)(2,1)} async-done(((bf16[256,512]{1,0:T(8,128)(2,1)}), bf16[256,4096]{1,0:T(8,128)(2,1)}) %all-gather.10.cloned.1.call-update) | async-done | bytes 2097168 | tf_op jit(solution)/shard_map/all_gather | solution.py:46
  432.7 4.6 convolution_multiply_fusion.2
  437.3 56.5 %all-gather.18.cloned.1.call-done = bf16[4096,256]{1,0:T(8,128)(2,1)} async-done(((bf16[512,256]{1,0:T(8,128)(2,1)}), bf16[4096,256]{1,0:T(8,128)(2,1)}) %all-gather.18.cloned.1.call-update) | async-done | bytes 2097168 | tf_op jit(solution)/shard_map/all_gather | solution.py:39
  493.8 3.8 multiply_convert_fusion
  497.6 57.3 %all-gather.16.cloned.1.call-done = bf16[4096,256]{1,0:T(8,128)(2,1)} async-done(((bf16[512,256]{1,0:T(8,128)(2,1)}), bf16[4096,256]{1,0:T(8,128)(2,1)}) %all-gather.16.cloned.1.call-update) | async-done | bytes 2097168 | tf_op jit(solution)/shard_map/all_gather | solution.py:34
  554.9 3.8 fusion
  558.7 57.4 %all-gather.12.cloned.1.call-done = bf16[4096,256]{1,0:T(8,128)(2,1)} async-done(((bf16[512,256]{1,0:T(8,128)(2,1)}), bf16[4096,256]{1,0:T(8,128)(2,1)}) %all-gather.12.cloned.1.call-update) | async-done | bytes 2097168 | tf_op jit(solution)/shard_map/all_gather | solution.py:40
  616.1 3.2 fusion.3
  619.3 4.4 convolution_convert_fusion
  623.7 199.1 %all-reduce.2.cloned.1.call-done = bf16[4096,512]{1,0:T(8,128)(2,1)} async-done(((bf16[4096,512]{1,0:T(8,128)(2,1)}), bf16[4096,512]{1,0:T(8,128)(2,1)}) %all-reduce.2.cloned.1.call-update) | async-done | bytes 4194320 | tf_op jit(solution)/shard_map/psum | solution.py:63
  822.8 1.2 dynamic-slice_convert_fusion
  823.9 1.1 fusion.14
  (13 shorter events, 1.4 us)
Async XLA Ops:
  7.2 160.2 %all-gather.20.cloned.1.call-start = ((), (), s32[]{:S(2)}) async-start(), calls=%async_computation.6 | async-start | bytes 4259840 | tf_op jit(solution)/shard_map/all_gather | solution.py:17
  9.8 306.4 %all-gather.22.cloned.1.call-start = ((), (), s32[]{:S(2)}) async-start(), calls=%async_computation.7 | async-start | bytes 4259840 | tf_op jit(solution)/shard_map/all_gather | solution.py:18
  10.5 361.1 %all-gather.14.cloned.1.call-start = ((), (), s32[]{:S(2)}) async-start(), calls=%async_computation.2 | async-start | bytes 2359296 | tf_op jit(solution)/shard_map/all_gather | solution.py:33
  11.3 421.4 %all-gather.10.cloned.1.call-start = ((), (), s32[]{:S(2)}) async-start(), calls=%async_computation | async-start | bytes 2359296 | tf_op jit(solution)/shard_map/all_gather | solution.py:46
  11.8 481.9 %all-gather.18.cloned.1.call-start = ((), (), s32[]{:S(2)}) async-start(), calls=%async_computation.4 | async-start | bytes 2359296 | tf_op jit(solution)/shard_map/all_gather | solution.py:39
  12.4 542.4 %all-gather.16.cloned.1.call-start = ((), (), s32[]{:S(2)}) async-start(), calls=%async_computation.3 | async-start | bytes 2359296 | tf_op jit(solution)/shard_map/all_gather | solution.py:34
  13.0 603.1 %all-gather.12.cloned.1.call-start = ((), (), s32[]{:S(2)}) async-start(), calls=%async_computation.1 | async-start | bytes 2359296 | tf_op jit(solution)/shard_map/all_gather | solution.py:40
  13.8 809.0 %all-reduce.2.cloned.1.call-start = ((), (), s32[]{:S(2)}) async-start(), calls=%async_computation.5 | async-start | bytes 8388608 | tf_op jit(solution)/shard_map/psum | solution.py:63
Sparse Core Ops, SparseCore 0:
  11.9 155.4 all-gather.19
  170.7 145.4 all-gather.21
  318.2 53.3 all-gather.13
  373.6 59.1 all-gather.9
  434.6 59.1 all-gather.17
  495.7 59.1 all-gather.15
  556.9 59.1 all-gather.11
  623.8 198.8 all-reduce.1
where the time goes:
time: 832 us
  waiting for transfers between devices  779 us (94%)
  matrix products  23.4 us (3%)
  between operations  14.2 us (2%)
  local copies, waits for them, and re-layouts  10.9 us (1%)
    psum x1, waiting for transfers between devices, per_device(): summed = lax.psum(full.astype(jnp.bfloat16), 'dp').astype(jnp.float32)  199 us
    all_gather x1, waiting for transfers between devices, per_device(): lax.all_gather(local, 'fsdp', axis=0, tiled=True)  154 us
    all_gather x1, waiting for transfers between devices, per_device(): lax.all_gather(out_grad, 'fsdp', axis=0, tiled=True)  145 us
    all_gather x1, waiting for transfers between devices, per_device(): lax.all_gather(w_down, 'dp', axis=1, tiled=True)  57.5 us
    all_gather x1, waiting for transfers between devices, per_device(): lax.all_gather(probe_up, 'dp', axis=0, tiled=True)  57.4 us
    all_gather x1, waiting for transfers between devices, per_device(): lax.all_gather(w_up, 'dp', axis=0, tiled=True)  57.3 us
    all_gather x1, waiting for transfers between devices, per_device(): lax.all_gather(probe_gate, 'dp', axis=0, tiled=True)  56.5 us
    all_gather x1, waiting for transfers between devices, per_device(): lax.all_gather(w_gate, 'dp', axis=0, tiled=True)  49.7 us
  transfers between devices with their start and end apart: 8, of which 8 were waited for; matrix products, arithmetic and copies ran while one was open for 3% of the time, Pallas kernels for 0%

commit v1 on v0

v1 whole, which is shorter than its diff:
```python
import functools

import jax
import jax.numpy as jnp
from jax import lax
from jax.experimental import pallas as pl
from jax.experimental.pallas import tpu as pltpu
from jax.sharding import PartitionSpec as P

MESH = pl.DeviceIdType.MESH
F32, BF16 = jnp.float32, jnp.bfloat16

NX, NY, NZ, NC = 4, 2, 16, 2
PEERS = NX * NY * NC
ROWS = 6
BLOCK = PEERS * ROWS
SLICE = 512
PAIRS = NZ // 2
UNIT = 2 * BLOCK
SHARE = UNIT // NX
STACK = 5 * SHARE
TOP = 128
HB = 128
LAG = 4


def kernel(
    blocks,
    scale,
    tokens,
    w_gate,
    w_up,
    probe_gate,
    probe_up,
    w_down,
    grads,
    out_gate,
    out_up,
    both,
    parcels,
    landed,
    tok,
    wide,
    down,
    part,
    via_left,
    via_right,
    from_left,
    from_right,
    tq,
    total,
    half_out,
    half_in,
    a2a_s,
    a2a_r,
    z_s,
    z_r,
    c_s,
    c_r,
    w_l,
    w_s,
    w_r,
    x_s,
    x_r,
    o_s,
    o_r,
):
    dp, fsdp = lax.axis_index("dp"), lax.axis_index("fsdp")
    x, yl = dp // 2, dp % 2
    yh, z, c = fsdp // 32, (fsdp // 2) % NZ, fsdp % 2
    units = blocks * PAIRS

    def device(x_, yl_, yh_, z_, c_):
        return (x_ * 2 + yl_, yh_ * 32 + z_ * 2 + c_)

    xr, xl, xo = (x + 1) % NX, (x + 3) % NX, (x + 2) % NX
    zr, zl = (z + 1) % NZ, (z + NZ - 1) % NZ
    right, left = device(xr, yl, yh, z, c), device(xl, yl, yh, z, c)
    above, below = device(x, yl, yh, zr, c), device(x, yl, yh, zl, c)
    other = device(x, yl, yh, z, 1 - c)
    mate = device(x, 1 - yl, yh, z, c)
    me = x * 4 + yh * 2 + c

    def peer(index):
        return device(index // 4, yl, (index // 2) % 2, z, index % 2)

    def remote(src, dst, send, recv, to):
        return pltpu.make_async_remote_copy(
            src_ref=src, dst_ref=dst, send_sem=send, recv_sem=recv, device_id=to, device_id_type=MESH
        )

    barrier = pltpu.get_barrier_semaphore()

    def greet(k, carry):
        pl.semaphore_signal(barrier, inc=1, device_id=peer((me + k) % PEERS), device_id_type=MESH)
        return carry

    lax.fori_loop(1, PEERS, greet, 0)
    for to in (above, below, mate):
        pl.semaphore_signal(barrier, inc=1, device_id=to, device_id_type=MESH)

    mats = (w_gate, w_up, probe_gate, probe_up)

    def weight_parts(j, slot):
        cols = pl.ds(j * HB, HB)
        pairs = [(m.at[:, cols], wide.at[slot, j, :, pl.ds(i * HB, HB)]) for i, m in enumerate(mats)]
        return pairs + [(w_down.at[cols, :], down.at[slot, j])]

    def own_copies(j):
        return [pltpu.make_async_copy(s, d, w_l.at[j, i]) for i, (s, d) in enumerate(weight_parts(j, yl))]

    def weight_sends(j):
        return [remote(s, d, w_s.at[j, i], w_r.at[j, i], mate) for i, (s, d) in enumerate(weight_parts(j, yl))]

    def weight_recvs(j):
        return [
            remote(d, d, w_s.at[j, i], w_r.at[j, i], mate)
            for i, (s, d) in enumerate(weight_parts(j, 1 - yl))
        ]

    for j in range(blocks):
        for copy in own_copies(j):
            copy.start()

    values = tokens[...].astype(F32)
    inverse = lax.rsqrt(jnp.mean(values * values, axis=1, keepdims=True) + 1e-05)
    both[...] = jnp.zeros_like(both)
    both[0:ROWS, :] = (values * inverse).astype(BF16).astype(F32)
    both[8 : 8 + ROWS, :] = grads[...].astype(F32)
    for q in range(8):
        parcels[q] = both[:, q * SLICE : (q + 1) * SLICE].astype(BF16)
    landed[me] = parcels[x * 2 + c]

    pl.semaphore_wait(barrier, PEERS - 1 + 3)

    def parcel(k):
        to = (me + k) % PEERS
        return remote(
            parcels.at[(to // 4) * 2 + to % 2], landed.at[me], a2a_s.at[k], a2a_r.at[k], peer(to)
        )

    def parcel_in(k):
        src = (me + PEERS - k) % PEERS
        return remote(landed.at[src], landed.at[src], a2a_s.at[k], a2a_r.at[k], peer(src))

    def start_parcel(k, carry):
        parcel(k).start()
        return carry

    def wait_parcel(k, carry):
        parcel_in(k).wait_recv()
        return carry

    lax.fori_loop(1, PEERS, start_parcel, 0)
    for copy in weight_sends(0):
        copy.start()
    lax.fori_loop(1, PEERS, wait_parcel, 0)

    col = lax.broadcasted_iota(jnp.int32, (2 * BLOCK, PEERS * 16), 1)
    row = lax.broadcasted_iota(jnp.int32, (2 * BLOCK, PEERS * 16), 0)
    source, place = col >> 4, col & 15
    kind, token = place >> 3, place & 7
    pick = (row == kind * BLOCK + source * ROWS + token) & (token < ROWS)
    packed = jnp.dot(
        jnp.where(pick, 1.0, 0.0).astype(BF16),
        landed[...].reshape(PEERS * 16, SLICE),
        preferred_element_type=F32,
    ).astype(BF16)
    tok[0, c, 0, 0] = packed[:BLOCK]
    tok[0, c, 1, 0] = packed[BLOCK:]

    def z_send(s, way, kind):
        src = tok.at[s, c, kind, way]
        if isinstance(s, int):
            src = tok.at[0, c, kind, 0]
        return remote(
            src,
            tok.at[s + 1, c, kind, way],
            z_s.at[s, way, kind],
            z_r.at[s + 1, way, kind],
            (above, below)[way],
        )

    def z_last(way):
        return remote(
            tok.at[PAIRS - 1, c, way, way],
            tok.at[0, c, way, 1],
            z_s.at[PAIRS - 1, way, way],
            z_r.at[0, 1, way],
            (above, below)[way],
        )

    def z_in(s, way, kind):
        return remote(tok.at[s, c, kind, way], tok.at[s, c, kind, way], z_s.at[s, way, kind], z_r.at[s, way, kind], above)

    def c_send(s, way, kind):
        piece = tok.at[s, c, kind, way]
        return remote(piece, piece, c_s.at[s, way, kind], c_r.at[s, way, kind], other)

    def c_in(s, way, kind):
        piece = tok.at[s, 1 - c, kind, way]
        return remote(piece, piece, c_s.at[s, way, kind], c_r.at[s, way, kind], other)

    for kind in range(2):
        for way in range(2):
            z_send(0, way, kind).start()
    for kind in range(2):
        c_send(0, 0, kind).start()

    def tokens_of(u):
        s = u + 1

        @pl.when(s < PAIRS)
        def _():
            for kind in range(2):
                for way in range(2):
                    z_in(s, way, kind).wait_recv()

                    @pl.when(s < PAIRS - 1)
                    def _(way=way, kind=kind):
                        z_send(s, way, kind).start()

                    if way == kind:

                        @pl.when(s == PAIRS - 1)
                        def _(way=way):
                            z_last(way).start()

                    c_send(s, way, kind).start()
            for kind in range(2):
                for way in range(2):
                    c_in(s, way, kind).wait_recv()

        @pl.when(s == PAIRS)
        def _():
            for kind in range(2):
                z_in(0, 1, kind).wait_recv()
                c_send(0, 1, kind).start()
            for kind in range(2):
                for way in range(2):
                    c_in(0, way, kind).wait_recv()

    bottom = STACK - TOP

    def x_copy(u, k, src, dst, to):
        return remote(src, dst, x_s.at[u, k], x_r.at[u, k], to)

    def scatter_sends(u):
        return [
            x_copy(u, 0, part.at[u, xo, pl.ds(0, TOP)], via_left.at[u], right),
            x_copy(u, 1, part.at[u, xo, pl.ds(TOP, bottom)], via_right.at[u], left),
            x_copy(u, 2, part.at[u, xr, pl.ds(TOP, bottom)], from_left.at[u, pl.ds(TOP, bottom)], right),
            x_copy(u, 3, part.at[u, xl, pl.ds(0, TOP)], from_right.at[u, pl.ds(0, TOP)], left),
        ]

    def mixed_sends(u):
        return [
            x_copy(u, 4, via_left.at[u], from_left.at[u, pl.ds(0, TOP)], right),
            x_copy(u, 5, via_right.at[u], from_right.at[u, pl.ds(TOP, bottom)], left),
        ]

    def tq_sends(u):
        return [
            x_copy(u, 6, tq.at[u, :, x], tq.at[u, :, x], right),
            x_copy(u, 7, tq.at[u, :, x], tq.at[u, :, x], left),
        ]

    def tq_ins(u):
        return [
            x_copy(u, 6, tq.at[u, :, xl], tq.at[u, :, xl], right),
            x_copy(u, 7, tq.at[u, :, xr], tq.at[u, :, xr], left),
        ]

    def tq_forwards(u):
        return [
            x_copy(u, 8, tq.at[u, 0, xl], tq.at[u, 0, xl], right),
            x_copy(u, 9, tq.at[u, 1, xr], tq.at[u, 1, xr], left),
        ]

    def tq_forward_ins(u):
        return [
            x_copy(u, 8, tq.at[u, 0, xo], tq.at[u, 0, xo], right),
            x_copy(u, 9, tq.at[u, 1, xo], tq.at[u, 1, xo], left),
        ]

    def products(u):
        j, i = u // PAIRS, u % PAIRS
        s = (i + 1) % PAIRS
        gates = jnp.zeros((UNIT, 4 * HB), F32)
        dhid = jnp.zeros((UNIT, HB), F32)
        for h in range(2):
            a = tok[s, h, 0].reshape(UNIT, SLICE)
            g = tok[s, h, 1].reshape(UNIT, SLICE)
            gates = gates + jnp.dot(a, wide[h, j], preferred_element_type=F32)
            dhid = dhid + lax.dot_general(g, down[h, j], (((1,), (1,)), ((), ())), preferred_element_type=F32)
        for q in range(NX):
            rows = slice(q * SHARE, (q + 1) * SHARE)
            for m in range(4):
                part[u, q, m * SHARE : (m + 1) * SHARE, :] = gates[rows, m * HB : (m + 1) * HB].astype(BF16)
            part[u, q, 4 * SHARE :, :] = (dhid[rows] * scale).astype(BF16)
        for copy in scatter_sends(u):
            copy.start()

    def mix(u):
        first, second = scatter_sends(u)[:2]
        first.wait_recv()
        via_left[u] = (via_left[u].astype(F32) + part[u, xr, :TOP].astype(F32)).astype(BF16)
        mixed_sends(u)[0].start()
        second.wait_recv()
        via_right[u] = (via_right[u].astype(F32) + part[u, xl, TOP:].astype(F32)).astype(BF16)
        mixed_sends(u)[1].start()

    def hidden(u):
        for copy in scatter_sends(u)[2:] + mixed_sends(u):
            copy.wait_recv()
        stack = part[u, x].astype(F32) + from_left[u].astype(F32) + from_right[u].astype(F32)
        gate, up, tgate, tup, dhid = (stack[m * SHARE : (m + 1) * SHARE] for m in range(5))
        sig = jax.nn.sigmoid(gate)
        first = sig * (1.0 + gate * (1.0 - sig))
        second = sig * (1.0 - sig) * (2.0 + gate * (1.0 - 2.0 * sig))
        tq[u, 0, x] = (dhid * (tup * first + up * second * tgate)).astype(BF16)
        tq[u, 1, x] = (dhid * first * tgate).astype(BF16)
        for copy in tq_sends(u):
            copy.start()

    def pass_on(u):
        for arrival, forward in zip(tq_ins(u), tq_forwards(u)):
            arrival.wait_recv()
            forward.start()

    def out_send(j):
        return remote(half_out.at[j], half_in.at[j], o_s.at[j], o_r.at[j], mate)

    def finish(u):
        j, i = u // PAIRS, u % PAIRS
        s = (i + 1) % PAIRS
        for copy in tq_forward_ins(u):
            copy.wait_recv()
        t = jnp.concatenate([tq[u, 0].reshape(UNIT, HB), tq[u, 1].reshape(UNIT, HB)], axis=1)
        for h in range(2):
            a = tok[s, h, 0].reshape(UNIT, SLICE)
            term = lax.dot_general(a, t, (((0,), (0,)), ((), ())), preferred_element_type=F32)

            @pl.when(i == 0)
            def _(h=h, term=term):
                total[j, h] = term

            @pl.when(i > 0)
            def _(h=h, term=term):
                total[j, h] += term

        @pl.when(i == PAIRS - 1)
        def _():
            half_out[j] = total[j, 1 - yl].astype(BF16)
            out_send(j).start()

        for copy in scatter_sends(u) + mixed_sends(u) + tq_sends(u) + tq_forwards(u):
            copy.wait_send()

    def step(n, carry):
        @pl.when(n < PAIRS)
        def _():
            tokens_of(n)

        for j in range(blocks):

            @pl.when(n == j * PAIRS)
            def _(j=j):
                for copy in own_copies(j):
                    copy.wait()
                for copy in weight_recvs(j):
                    copy.wait_recv()
                if j + 1 < blocks:
                    for copy in weight_sends(j + 1):
                        copy.start()

        for lag, stage in enumerate((products, mix, hidden, pass_on, finish)):

            @pl.when((n >= lag) & (n < units + lag))
            def _(lag=lag, stage=stage):
                stage(n - lag)

        return carry

    lax.fori_loop(0, units + LAG, step, 0)

    for j in range(blocks):
        out_send(j).wait_recv()
        mine = total[j, yl] + half_in[j].astype(F32)
        out_gate[:, j * HB : (j + 1) * HB] = mine[:, :HB]
        out_up[:, j * HB : (j + 1) * HB] = mine[:, HB:]

    def sent_parcel(k, carry):
        parcel(k).wait_send()
        return carry

    lax.fori_loop(1, PEERS, sent_parcel, 0)

    def sent_pieces(s, carry):
        for kind in range(2):
            for way in range(2):

                @pl.when(s < PAIRS - 1)
                def _(way=way, kind=kind):
                    z_send(s, way, kind).wait_send()

                c_send(s, way, kind).wait_send()
        return carry

    lax.fori_loop(0, PAIRS, sent_pieces, 0)
    for way in range(2):
        z_last(way).wait_send()
    for j in range(blocks):
        for copy in weight_sends(j):
            copy.wait_send()
        out_send(j).wait_send()


def per_device(tokens, w_gate, w_up, probe_gate, probe_up, w_down, out_grad):
    width = w_gate.shape[1]
    blocks = width // HB
    units = blocks * PAIRS
    everywhere = lax.axis_size("dp") * lax.axis_size("fsdp")
    scale = 1.0 / float(tokens.shape[0] * everywhere) ** 0.5
    dma = pltpu.SemaphoreType.DMA
    vmem, any_ = pl.BlockSpec(memory_space=pltpu.VMEM), pl.BlockSpec(memory_space=pl.ANY)
    return pl.pallas_call(
        functools.partial(kernel, blocks, scale),
        out_shape=(jax.ShapeDtypeStruct((SLICE, width), F32),) * 2,
        in_specs=[vmem] + [any_] * 5 + [vmem],
        out_specs=(vmem, vmem),
        scratch_shapes=[
            pltpu.VMEM((16, 8 * SLICE), F32),
            pltpu.VMEM((8, 16, SLICE), BF16),
            pltpu.VMEM((PEERS, 16, SLICE), BF16),
            pltpu.VMEM((PAIRS, 2, 2, 2, BLOCK, SLICE), BF16),
            pltpu.VMEM((2, blocks, SLICE, 4 * HB), BF16),
            pltpu.VMEM((2, blocks, HB, SLICE), BF16),
            pltpu.VMEM((units, NX, STACK, HB), BF16),
            pltpu.VMEM((units, TOP, HB), BF16),
            pltpu.VMEM((units, STACK - TOP, HB), BF16),
            pltpu.VMEM((units, STACK, HB), BF16),
            pltpu.VMEM((units, STACK, HB), BF16),
            pltpu.VMEM((units, 2, NX, SHARE, HB), BF16),
            pltpu.VMEM((blocks, 2, SLICE, 2 * HB), F32),
            pltpu.VMEM((blocks, SLICE, 2 * HB), BF16),
            pltpu.VMEM((blocks, SLICE, 2 * HB), BF16),
            dma((PEERS,)),
            dma((PEERS,)),
            dma((PAIRS, 2, 2)),
            dma((PAIRS, 2, 2)),
            dma((PAIRS, 2, 2)),
            dma((PAIRS, 2, 2)),
            dma((blocks, 5)),
            dma((blocks, 5)),
            dma((blocks, 5)),
            dma((units, 10)),
            dma((units, 10)),
            dma((blocks,)),
            dma((blocks,)),
        ],
        compiler_params=pltpu.CompilerParams(
            collective_id=0, has_side_effects=True, vmem_limit_bytes=48 * 1024 * 1024
        ),
    )(tokens, w_gate, w_up, probe_gate, probe_up, w_down, out_grad)


def solution(mesh):
    placed = (
        P(("dp", "fsdp"), None),
        P("dp", "fsdp"),
        P("dp", "fsdp"),
        P("dp", "fsdp"),
        P("dp", "fsdp"),
        P("fsdp", "dp"),
        P(("dp", "fsdp"), None),
    )
    return jax.shard_map(
        per_device,
        mesh=mesh,
        in_specs=placed,
        out_specs=(P("dp", "fsdp"), P("dp", "fsdp")),
        check_vma=False,
    )
```

time: 832 us -> 124 us (0.15)
  the two profiles are of different devices: /device:TPU:4 before, /device:TPU:2 now
where the time goes in v1:
time: 124 us
  Pallas kernels  115 us (93%)
  local copies, waits for them, and re-layouts  8.01 us (6%)
    pallas_call x1, Pallas kernels, per_device(): pl.pallas_call(functools.partial(kernel, blocks, scale), out_shape=(jax.S...  115 us
    unnamed x16, local copies, waits for them, and re-layouts  8.01 us

profile of v1, /device:TPU:2, one launch (start us, length us, event | category | flops | bytes accessed | tf_op | source)
XLA Modules:
  0.0 123.5 jit_solution(1278424960100726951)
XLA Ops:
  0.6 0.0 copy-start
  0.6 0.9 copy-done
  1.6 0.0 copy-start.1
  1.6 0.9 copy-done.1
  2.5 0.0 copy-start.2
  2.5 0.9 copy-done.2
  3.5 0.0 copy-start.3
  3.5 0.9 copy-done.3
  4.4 0.0 copy-start.4
  4.4 0.9 copy-done.4
  5.4 0.0 copy-start.5
  5.4 0.8 copy-done.5
  6.2 0.0 copy-start.6
  6.2 0.8 copy-done.6
  7.1 114.8 %shard_map.86 = (f32[512,256]{1,0:T(8,128)S(1)}, f32[512,256]{1,0:T(8,128)S(1)}) custom-call(bf16[6,4096]{1,0:T(8,128)(2,1)S(1)} %copy-done.5, bf16[512,256]{1,0:T(8,128)(2,1)S(1)} %copy-done, bf16[512,256]{1,0:T(8,128)(2,1)S(1)} %copy-done.1, bf16[512,256]{1,0:T(8,128)(2,1)S(1)} %copy-done.2, bf16[512,256]{1,0:T(8,128)(2,1)S(1)} %copy-done.3, ...), custom_call_target="tpu_custom_call" | custom-call | tf_op jit(solution)/shard_map/pallas_call | solution.py:427
  121.9 0.8 copy.11
  122.7 0.8 copy.12
Async XLA Ops:
  0.6 1.0 copy-start
  1.6 0.9 copy-start.1
  2.5 0.9 copy-start.2
  3.5 0.9 copy-start.3
  4.4 0.9 copy-start.4
  5.4 0.8 copy-start.5
  6.2 0.8 copy-start.6

commit v2 on v1

v2 whole, which is shorter than its diff:
```python
import functools

import jax
import jax.numpy as jnp
from jax import lax
from jax.experimental import pallas as pl
from jax.experimental.pallas import tpu as pltpu
from jax.sharding import PartitionSpec as P

MESH = pl.DeviceIdType.MESH
F32, BF16 = jnp.float32, jnp.bfloat16

NX, NY, NZ, NC = 4, 2, 16, 2
PEERS = NX * NY * NC
ROWS = 6
BLOCK = PEERS * ROWS
SLICE = 512
PAIRS = NZ // 2
UNIT = 2 * BLOCK
SHARE = UNIT // NX
STACK = 5 * SHARE
TOP = 128
HB = 128
LAG = 4
DIRECT = 2
SLOTS = 8
CUTS = 2
PIECE = BLOCK // CUTS
AHEAD = 4
TICKS = 2 * CUTS * PAIRS


def kernel(
    blocks,
    scale,
    tokens,
    w_gate,
    w_up,
    probe_gate,
    probe_up,
    w_down,
    grads,
    own_gate,
    own_up,
    in_gate,
    in_up,
    both,
    parcels,
    landed,
    tok,
    wide,
    down,
    part,
    via,
    from_left,
    from_right,
    tq,
    total,
    half_out,
    a2a_s,
    a2a_r,
    z_s,
    z_last_s,
    z_r,
    c_s,
    c_r,
    w_l,
    w_s,
    w_r,
    x_s,
    x_r,
    o_s,
    o_r,
    o_l,
):
    dp, fsdp = lax.axis_index("dp"), lax.axis_index("fsdp")
    x, yl = dp // 2, dp % 2
    yh, z, c = fsdp // 32, (fsdp // 2) % NZ, fsdp % 2
    units = blocks * PAIRS

    def device(x_, yl_, yh_, z_, c_):
        return (x_ * 2 + yl_, yh_ * 32 + z_ * 2 + c_)

    xr, xl, xo = (x + 1) % NX, (x + 3) % NX, (x + 2) % NX
    zr, zl = (z + 1) % NZ, (z + NZ - 1) % NZ
    right, left = device(xr, yl, yh, z, c), device(xl, yl, yh, z, c)
    above, below = device(x, yl, yh, zr, c), device(x, yl, yh, zl, c)
    other = device(x, yl, yh, z, 1 - c)
    mate = device(x, 1 - yl, yh, z, c)
    me = x * 4 + yh * 2 + c

    def peer(index):
        return device(index // 4, yl, (index // 2) % 2, z, index % 2)

    def remote(src, dst, send, recv, to):
        return pltpu.make_async_remote_copy(
            src_ref=src, dst_ref=dst, send_sem=send, recv_sem=recv, device_id=to, device_id_type=MESH
        )

    barrier = pltpu.get_barrier_semaphore()

    def greet(k, carry):
        pl.semaphore_signal(barrier, inc=1, device_id=peer((me + k) % PEERS), device_id_type=MESH)
        return carry

    lax.fori_loop(1, PEERS, greet, 0)
    for to in (above, below, mate):
        pl.semaphore_signal(barrier, inc=1, device_id=to, device_id_type=MESH)

    mats = (w_gate, w_up, probe_gate, probe_up)

    def weight_parts(j, slot):
        cols = pl.ds(j * HB, HB)
        pairs = [(m.at[:, cols], wide.at[slot, j, :, pl.ds(i * HB, HB)]) for i, m in enumerate(mats)]
        return pairs + [(w_down.at[cols, :], down.at[slot, j])]

    def own_copies(j):
        return [
            pltpu.make_async_copy(s, d, w_l.at[j, i // 4]) for i, (s, d) in enumerate(weight_parts(j, yl))
        ]

    def weight_sends(j):
        return [
            remote(s, d, w_s.at[j, i // 4], w_r.at[j, i // 4], mate)
            for i, (s, d) in enumerate(weight_parts(j, yl))
        ]

    def weights_whole(j, slot):
        return [
            remote(ref.at[slot, j], ref.at[slot, j], w_s.at[j, i], w_r.at[j, i], mate)
            for i, ref in enumerate((wide, down))
        ]

    def own_whole(j):
        return [
            pltpu.make_async_copy(ref.at[yl, j], ref.at[yl, j], w_l.at[j, i])
            for i, ref in enumerate((wide, down))
        ]

    for j in range(blocks):
        for copy in own_copies(j):
            copy.start()

    values = tokens[...].astype(F32)
    inverse = lax.rsqrt(jnp.mean(values * values, axis=1, keepdims=True) + 1e-05)
    both[...] = jnp.zeros_like(both)
    both[0:ROWS, :] = (values * inverse).astype(BF16).astype(F32)
    both[8 : 8 + ROWS, :] = grads[...].astype(F32)
    for q in range(8):
        parcels[q] = both[:, q * SLICE : (q + 1) * SLICE].astype(BF16)
    landed[me] = parcels[x * 2 + c]

    pl.semaphore_wait(barrier, PEERS - 1 + 3)

    def start_parcel(k, carry):
        to = (me + k) % PEERS
        remote(
            parcels.at[(to // 4) * 2 + to % 2], landed.at[me], a2a_s.at[0], a2a_r.at[0], peer(to)
        ).start()
        return carry

    lax.fori_loop(1, PEERS, start_parcel, 0)
    for copy in weight_sends(0):
        copy.start()
    parcels_whole = remote(
        landed.at[pl.ds(0, PEERS - 1)], landed.at[pl.ds(0, PEERS - 1)], a2a_s.at[0], a2a_r.at[0], other
    )
    parcels_whole.wait_recv()

    col = lax.broadcasted_iota(jnp.int32, (2 * BLOCK, PEERS * 16), 1)
    row = lax.broadcasted_iota(jnp.int32, (2 * BLOCK, PEERS * 16), 0)
    source, place = col >> 4, col & 15
    kind, token = place >> 3, place & 7
    pick = (row == kind * BLOCK + source * ROWS + token) & (token < ROWS)
    packed = jnp.dot(
        jnp.where(pick, 1.0, 0.0).astype(BF16),
        landed[...].reshape(PEERS * 16, SLICE),
        preferred_element_type=F32,
    ).astype(BF16)
    tok[0, c, 0, 0] = packed[:BLOCK].reshape(CUTS, PIECE, SLICE)
    tok[0, c, 1, 0] = packed[BLOCK:].reshape(CUTS, PIECE, SLICE)

    def z_send(s, way, kind, cut):
        src = tok.at[s, c, kind, 0 if isinstance(s, int) else way, cut]
        return remote(
            src, tok.at[s + 1, c, kind, way, cut], z_s.at[0], z_r.at[s + 1, way, kind, cut], (above, below)[way]
        )

    def z_last(way, cut):
        to = device(x, yl, yh, (z + 1 + way * (NZ - 2)) % NZ, c)
        src, dst = tok.at[PAIRS - 1, c, way, way, cut], tok.at[0, c, way, 1, cut]
        return remote(src, dst, z_last_s.at[0], z_r.at[0, 1, way, cut], to)

    def z_in(s, way, kind, cut):
        piece = tok.at[s, c, kind, way, cut]
        return remote(piece, piece, z_s.at[0], z_r.at[s, way, kind, cut], above)

    def c_send(s, way, kind):
        piece = tok.at[s, c, kind, way]
        return remote(piece, piece, c_s.at[0], c_r.at[s], other)

    def c_in(s):
        return remote(tok.at[s, 1 - c], tok.at[s, 1 - c], c_s.at[0], c_r.at[s], other)

    for kind in range(2):
        for cut in range(CUTS):
            for way in range(2):
                z_send(0, way, kind, cut).start()
    for kind in range(2):
        c_send(0, 0, kind).start()

    def tick(k, carry=None):
        s, kind, cut = k // (2 * CUTS) + 1, (k // CUTS) % 2, k % CUTS

        @pl.when(s < PAIRS)
        def _():
            for way in range(2):
                z_in(s, way, kind, cut).wait_recv()

                @pl.when(s < PAIRS - 1)
                def _(way=way):
                    z_send(s, way, kind, cut).start()

            @pl.when(s == PAIRS - 1)
            def _():
                z_last(kind, cut).start()

            @pl.when(cut == CUTS - 1)
            def _():
                for way in range(2):
                    c_send(s, way, kind).start()

        @pl.when(s == PAIRS)
        def _():
            z_in(0, 1, kind, cut).wait_recv()

            @pl.when(cut == CUTS - 1)
            def _():
                c_send(0, 1, kind).start()

        return carry

    lax.fori_loop(0, AHEAD, tick, 0)

    def place(n):
        quarter = n // (PAIRS // 2)
        mixed = ((quarter + 1) // 2) % 2
        last = quarter // 3
        j = mixed * (1 - n % 2) + last
        i = (1 - mixed - last) * n + mixed * (n // 2 - 2 + (n % 2) * 4) + last * (n - PAIRS)
        return j, i

    bottom = STACK - TOP

    F_LEFT, F_RIGHT, LEFT, RIGHT, T_LEFT, T_RIGHT, T_FAR = range(7)
    SCATTER, MIXED, TQ, PASSED = range(4)
    far = device(xo, yl, yh, z, c)

    def x_copy(u, send, recv, src, dst, to):
        slot = u % SLOTS
        return remote(src, dst, x_s.at[slot, send], x_r.at[slot, recv], to)

    def x_start(u, send, *copies):
        for recv, src, dst, to in copies:
            x_copy(u, send, recv, src, dst, to).start()

    def x_wait(u, recv, ref):
        x_copy(u, 0, recv, ref, ref, far).wait_recv()

    def x_sent(u, send, ref):
        x_copy(u, send, 0, ref, ref, far).wait_send()

    top, low = pl.ds(0, TOP), pl.ds(TOP, bottom)

    def ring(u):
        return u < units - DIRECT

    def products(u):
        j, i = place(u)
        s = (i + 1) % PAIRS
        gates = jnp.zeros((UNIT, 4 * HB), F32)
        dhid = jnp.zeros((UNIT, HB), F32)
        for h in range(2):
            a = tok[s, h, 0].reshape(UNIT, SLICE)
            g = tok[s, h, 1].reshape(UNIT, SLICE)
            gates = gates + jnp.dot(a, wide[h, j], preferred_element_type=F32)
            dhid = dhid + lax.dot_general(g, down[h, j], (((1,), (1,)), ((), ())), preferred_element_type=F32)
        for q in range(NX):
            rows = slice(q * SHARE, (q + 1) * SHARE)
            for m in range(4):
                part[u, q, m * SHARE : (m + 1) * SHARE, :] = gates[rows, m * HB : (m + 1) * HB].astype(BF16)
            part[u, q, 4 * SHARE :, :] = (dhid[rows] * scale).astype(BF16)

        @pl.when(ring(u))
        def _():
            x_start(
                u,
                SCATTER,
                (F_LEFT, part.at[u, xo, top], via.at[u, top], right),
                (F_RIGHT, part.at[u, xo, low], via.at[u, low], left),
                (LEFT, part.at[u, xr, low], from_left.at[u, low], right),
                (RIGHT, part.at[u, xl, top], from_right.at[u, top], left),
            )

        @pl.when(u >= units - DIRECT)
        def _():
            x_start(
                u,
                SCATTER,
                (F_LEFT, part.at[u, xo], via.at[u], far),
                (LEFT, part.at[u, xr], from_left.at[u], right),
                (RIGHT, part.at[u, xl], from_right.at[u], left),
            )

    def mix(u):
        @pl.when(ring(u))
        def _():
            x_wait(u, F_LEFT, via.at[u, top])
            via[u, :TOP] = (via[u, :TOP].astype(F32) + part[u, xr, :TOP].astype(F32)).astype(BF16)
            x_start(u, MIXED, (LEFT, via.at[u, top], from_left.at[u, top], right))
            x_wait(u, F_RIGHT, via.at[u, low])
            via[u, TOP:] = (via[u, TOP:].astype(F32) + part[u, xl, TOP:].astype(F32)).astype(BF16)
            x_start(u, MIXED, (RIGHT, via.at[u, low], from_right.at[u, low], left))

    def activate(u, stack):
        gate, up, tgate, tup, dhid = (stack[m * SHARE : (m + 1) * SHARE] for m in range(5))
        sig = jax.nn.sigmoid(gate)
        first = sig * (1.0 + gate * (1.0 - sig))
        second = sig * (1.0 - sig) * (2.0 + gate * (1.0 - 2.0 * sig))
        tq[u, 0, x] = (dhid * (tup * first + up * second * tgate)).astype(BF16)
        tq[u, 1, x] = (dhid * first * tgate).astype(BF16)
        x_start(
            u,
            TQ,
            (T_LEFT, tq.at[u, :, x], tq.at[u, :, x], right),
            (T_RIGHT, tq.at[u, :, x], tq.at[u, :, x], left),
        )

    def hidden(u):
        x_wait(u, LEFT, from_left.at[u])
        x_wait(u, RIGHT, from_right.at[u])

        @pl.when(ring(u))
        def _():
            activate(u, part[u, x].astype(F32) + from_left[u].astype(F32) + from_right[u].astype(F32))

        @pl.when(u >= units - DIRECT)
        def _():
            x_wait(u, F_LEFT, via.at[u])
            near = part[u, x].astype(F32) + from_left[u].astype(F32)
            activate(u, near + from_right[u].astype(F32) + via[u].astype(F32))
            x_start(u, TQ, (T_FAR, tq.at[u, :, x], tq.at[u, :, x], far))

    def pass_on(u):
        @pl.when(ring(u))
        def _():
            x_wait(u, T_LEFT, tq.at[u, :, xl])
            x_start(u, PASSED, (T_FAR, tq.at[u, 0, xl], tq.at[u, 0, xl], right))
            x_wait(u, T_RIGHT, tq.at[u, :, xr])
            x_start(u, PASSED, (T_FAR, tq.at[u, 1, xr], tq.at[u, 1, xr], left))

    def out_sends(j):
        cols = pl.ds(j * HB, HB)
        return [
            remote(half_out.at[j, g], ref.at[:, cols], o_s.at[j, g], o_r.at[j, g], mate)
            for g, ref in enumerate((in_gate, in_up))
        ]

    def out_copies(j):
        cols = pl.ds(j * HB, HB)
        return [
            pltpu.make_async_copy(total.at[j, yl, :, pl.ds(g * HB, HB)], ref.at[:, cols], o_l.at[j, g])
            for g, ref in enumerate((own_gate, own_up))
        ]

    def finish(u):
        j, i = place(u)
        s = (i + 1) % PAIRS

        @pl.when(u >= units - DIRECT)
        def _():
            x_wait(u, T_LEFT, tq.at[u, :, xl])
            x_wait(u, T_RIGHT, tq.at[u, :, xr])

        x_wait(u, T_FAR, tq.at[u, :, xo])
        t = jnp.concatenate([tq[u, 0].reshape(UNIT, HB), tq[u, 1].reshape(UNIT, HB)], axis=1)
        for h in (1 - yl, yl):
            a = tok[s, h, 0].reshape(UNIT, SLICE)
            term = lax.dot_general(a, t, (((0,), (0,)), ((), ())), preferred_element_type=F32)

            @pl.when(i == 0)
            def _(h=h, term=term):
                total[j, h] = term

            @pl.when(i > 0)
            def _(h=h, term=term):
                total[j, h] += term

            if h is not yl:
                for jj in range(blocks):

                    @pl.when((i == PAIRS - 1) & (j == jj))
                    def _(jj=jj):
                        for g, copy in enumerate(out_sends(jj)):
                            half_out[jj, g] = total[jj, 1 - yl, :, g * HB : (g + 1) * HB].astype(BF16)
                            copy.start()

        for jj in range(blocks):

            @pl.when((i == PAIRS - 1) & (j == jj))
            def _(jj=jj):
                for copy in out_copies(jj):
                    copy.start()

        @pl.when(ring(u))
        def _():
            x_sent(u, SCATTER, part.at[u, pl.ds(0, 2)])
            x_sent(u, MIXED, part.at[u, 0])
            x_sent(u, TQ, tq.at[u, :, pl.ds(0, 2)])
            x_sent(u, PASSED, tq.at[u, :, 0])

        @pl.when(u >= units - DIRECT)
        def _():
            x_sent(u, SCATTER, part.at[u, pl.ds(0, 3)])
            x_sent(u, TQ, tq.at[u, :, pl.ds(0, 3)])

    def step(n, carry):
        j, i = place(n)

        def ticks(lag):
            if lag in (0, 1, 2, 4):

                @pl.when(n < PAIRS // 2)
                def _():
                    tick(AHEAD + 4 * n + min(lag, 3))

            if lag in (0, 2):
                k = AHEAD + 4 * (PAIRS // 2) + 2 * (n - PAIRS // 2) + lag // 2

                @pl.when((n >= PAIRS // 2) & (k < TICKS))
                def _():
                    tick(k)

        ticks(0)

        @pl.when((n < 3 * PAIRS // 2) & (j == 0))
        def _():
            c_in((i + 1) % PAIRS).wait_recv()

        for jj in range(blocks):

            @pl.when(n == jj * (PAIRS // 2))
            def _(jj=jj):
                for copy in own_whole(jj):
                    copy.wait()
                for copy in weights_whole(jj, 1 - yl):
                    copy.wait_recv()
                if jj + 1 < blocks:
                    for copy in weight_sends(jj + 1):
                        copy.start()

        for lag, stage in enumerate((products, mix, hidden, pass_on, finish)):
            if lag:
                ticks(lag)

            @pl.when((n >= lag) & (n < units + lag))
            def _(lag=lag, stage=stage):
                stage(n - lag)

        return carry

    lax.fori_loop(0, units + LAG, step, 0)

    parcels_whole.wait_send()
    first_steps, half = tok.at[pl.ds(0, PAIRS - 1), c], tok.at[:, c]
    remote(first_steps, first_steps, z_s.at[0], z_r.at[0, 0, 0, 0], above).wait_send()
    remote(tok.at[0, c, 0], tok.at[0, c, 0], z_last_s.at[0], z_r.at[0, 0, 0, 0], above).wait_send()
    remote(half, half, c_s.at[0], c_r.at[0], other).wait_send()
    for j in range(blocks):
        for copy in weights_whole(j, yl):
            copy.wait_send()
        for copy in out_copies(j):
            copy.wait()
    for j in range(blocks):
        for copy in out_sends(j):
            copy.wait()


def per_device(tokens, w_gate, w_up, probe_gate, probe_up, w_down, out_grad):
    width = w_gate.shape[1]
    blocks = width // HB
    units = blocks * PAIRS
    everywhere = lax.axis_size("dp") * lax.axis_size("fsdp")
    scale = 1.0 / float(tokens.shape[0] * everywhere) ** 0.5
    dma = pltpu.SemaphoreType.DMA
    vmem, any_ = pl.BlockSpec(memory_space=pltpu.VMEM), pl.BlockSpec(memory_space=pl.ANY)
    own_gate, own_up, in_gate, in_up = pl.pallas_call(
        functools.partial(kernel, blocks, scale),
        out_shape=(jax.ShapeDtypeStruct((SLICE, width), F32),) * 2
        + (jax.ShapeDtypeStruct((SLICE, width), BF16),) * 2,
        in_specs=[vmem] + [any_] * 5 + [vmem],
        out_specs=(any_,) * 4,
        scratch_shapes=[
            pltpu.VMEM((16, 8 * SLICE), F32),
            pltpu.VMEM((8, 16, SLICE), BF16),
            pltpu.VMEM((PEERS, 16, SLICE), BF16),
            pltpu.VMEM((PAIRS, 2, 2, 2, CUTS, PIECE, SLICE), BF16),
            pltpu.VMEM((2, blocks, SLICE, 4 * HB), BF16),
            pltpu.VMEM((2, blocks, HB, SLICE), BF16),
            pltpu.VMEM((units, NX, STACK, HB), BF16),
            pltpu.VMEM((units, STACK, HB), BF16),
            pltpu.VMEM((units, STACK, HB), BF16),
            pltpu.VMEM((units, STACK, HB), BF16),
            pltpu.VMEM((units, 2, NX, SHARE, HB), BF16),
            pltpu.VMEM((blocks, 2, SLICE, 2 * HB), F32),
            pltpu.VMEM((blocks, 2, SLICE, HB), BF16),
            dma((1,)),
            dma((1,)),
            dma((1,)),
            dma((1,)),
            dma((PAIRS, 2, 2, CUTS)),
            dma((1,)),
            dma((PAIRS,)),
            dma((blocks, 2)),
            dma((blocks, 2)),
            dma((blocks, 2)),
            dma((SLOTS, 4)),
            dma((SLOTS, 7)),
            dma((blocks, 2)),
            dma((blocks, 2)),
            dma((blocks, 2)),
        ],
        compiler_params=pltpu.CompilerParams(
            collective_id=0, has_side_effects=True, vmem_limit_bytes=62 * 1024 * 1024
        ),
    )(tokens, w_gate, w_up, probe_gate, probe_up, w_down, out_grad)
    return own_gate + in_gate.astype(F32), own_up + in_up.astype(F32)


def solution(mesh):
    placed = (
        P(("dp", "fsdp"), None),
        P("dp", "fsdp"),
        P("dp", "fsdp"),
        P("dp", "fsdp"),
        P("dp", "fsdp"),
        P("fsdp", "dp"),
        P(("dp", "fsdp"), None),
    )
    return jax.shard_map(
        per_device,
        mesh=mesh,
        in_specs=placed,
        out_specs=(P("dp", "fsdp"), P("dp", "fsdp")),
        check_vma=False,
    )
```

time: 124 us -> 109 us (0.88)
  the two profiles are of different devices: /device:TPU:2 before, /device:TPU:32 now
where the time goes in v2:
time: 109 us; the launch traced here: 108 us
  Pallas kernels  105 us (96%)
  other arithmetic  2.42 us (2%)
    pallas_call x1, Pallas kernels, per_device(): pl.pallas_call(functools.partial(kernel, blocks, scale), out_shape=(jax.S...  105 us
    add x1, other arithmetic, per_device(): return (own_gate + in_gate.astype(F32), own_up + in_up.astype(F32))  2.42 us

profile of v2, /device:TPU:32, one launch (start us, length us, event | category | flops | bytes accessed | tf_op | source)
XLA Modules:
  0.0 108.3 jit_solution(11191212602841810270)
XLA Ops:
  0.6 105.3 %shard_map.86 = (f32[512,256]{1,0:T(8,128)}, f32[512,256]{1,0:T(8,128)}, bf16[512,256]{1,0:T(8,128)(2,1)}, bf16[512,256]{1,0:T(8,128)(2,1)}) custom-call(bf16[6,4096]{1,0:T(8,128)(2,1)} %tokens.1, bf16[512,256]{1,0:T(8,128)(2,1)} %w_gate.1, bf16[512,256]{1,0:T(8,128)(2,1)} %w_up.1, bf16[512,256]{1,0:T(8,128)(2,1)} %probe_gate.1, bf16[512,256]{1,0:T(8,128)(2,1)} %probe_up.1, ...), custom_call_target="tpu_custom_call" | custom-call | tf_op jit(solution)/shard_map/pallas_call | solution.py:497
  105.9 2.4 %convert_add_fusion = (f32[512,256]{1,0:T(8,128)}, f32[512,256]{1,0:T(8,128)}) fusion(f32[512,256]{1,0:T(8,128)} %get-tuple-element.8, bf16[512,256]{1,0:T(8,128)(2,1)} %get-tuple-element.9, f32[512,256]{1,0:T(8,128)} %get-tuple-element.6, bf16[512,256]{1,0:T(8,128)(2,1)} %get-tuple-element.7), kind=kLoop, calls=%fused_computation | loop fusion | flops 524288 | bytes 2621440 | tf_op jit(solution)/shard_map/add | solution.py:537

commit v3 on v2

--- a/solution.py
+++ b/solution.py
@@ -21,9 +21,9 @@
 STACK = 5 * SHARE
 TOP = 128
 HB = 128
-LAG = 4
-DIRECT = 2
-SLOTS = 8
+LAGS = (0, 2, 4, 6, 8)
+DIRECT = 0
+SLOTS = 10
 CUTS = 2
 PIECE = BLOCK // CUTS
 AHEAD = 4
@@ -427,15 +427,15 @@
     def step(n, carry):
         j, i = place(n)
 
-        def ticks(lag):
-            if lag in (0, 1, 2, 4):
+        def ticks(order):
+            if order in (0, 1, 2, 4):
 
                 @pl.when(n < PAIRS // 2)
                 def _():
-                    tick(AHEAD + 4 * n + min(lag, 3))
-
-            if lag in (0, 2):
-                k = AHEAD + 4 * (PAIRS // 2) + 2 * (n - PAIRS // 2) + lag // 2
+                    tick(AHEAD + 4 * n + min(order, 3))
+
+            if order in (2, 4):
+                k = AHEAD + 4 * (PAIRS // 2) + 2 * (n - PAIRS // 2) + (order - 2) // 2
 
                 @pl.when((n >= PAIRS // 2) & (k < TICKS))
                 def _():
@@ -459,9 +459,9 @@
                     for copy in weight_sends(jj + 1):
                         copy.start()
 
-        for lag, stage in enumerate((products, mix, hidden, pass_on, finish)):
-            if lag:
-                ticks(lag)
+        for order, (lag, stage) in enumerate(zip(LAGS, (products, mix, hidden, pass_on, finish))):
+            if order:
+                ticks(order)
 
             @pl.when((n >= lag) & (n < units + lag))
             def _(lag=lag, stage=stage):
@@ -469,7 +469,7 @@
 
         return carry
 
-    lax.fori_loop(0, units + LAG, step, 0)
+    lax.fori_loop(0, units + LAGS[-1], step, 0)
 
     parcels_whole.wait_send()
     first_steps, half = tok.at[pl.ds(0, PAIRS - 1), c], tok.at[:, c]

time: 109 us -> 104 us (0.954)
  the two profiles are of different devices: /device:TPU:32 before, /device:TPU:2 now
where the time goes in v3:
time: 104 us
  Pallas kernels  101 us (97%)
  other arithmetic  2.42 us (2%)
    pallas_call x1, Pallas kernels, per_device(): pl.pallas_call(functools.partial(kernel, blocks, scale), out_shape=(jax.S...  101 us
    add x1, other arithmetic, per_device(): return (own_gate + in_gate.astype(F32), own_up + in_up.astype(F32))  2.42 us

profile of v3, /device:TPU:2, one launch (start us, length us, event | category | flops | bytes accessed | tf_op | source)
XLA Modules:
  0.0 104.2 jit_solution(15542480844727458524)
XLA Ops:
  0.6 101.1 %shard_map.86 = (f32[512,256]{1,0:T(8,128)}, f32[512,256]{1,0:T(8,128)}, bf16[512,256]{1,0:T(8,128)(2,1)}, bf16[512,256]{1,0:T(8,128)(2,1)}) custom-call(bf16[6,4096]{1,0:T(8,128)(2,1)} %tokens.1, bf16[512,256]{1,0:T(8,128)(2,1)} %w_gate.1, bf16[512,256]{1,0:T(8,128)(2,1)} %w_up.1, bf16[512,256]{1,0:T(8,128)(2,1)} %probe_gate.1, bf16[512,256]{1,0:T(8,128)(2,1)} %probe_up.1, ...), custom_call_target="tpu_custom_call" | custom-call | tf_op jit(solution)/shard_map/pallas_call | solution.py:497
  101.7 2.4 %convert_add_fusion = (f32[512,256]{1,0:T(8,128)}, f32[512,256]{1,0:T(8,128)}) fusion(f32[512,256]{1,0:T(8,128)} %get-tuple-element.8, bf16[512,256]{1,0:T(8,128)(2,1)} %get-tuple-element.9, f32[512,256]{1,0:T(8,128)} %get-tuple-element.6, bf16[512,256]{1,0:T(8,128)(2,1)} %get-tuple-element.7), kind=kLoop, calls=%fused_computation | loop fusion | flops 524288 | bytes 2621440 | tf_op jit(solution)/shard_map/add | solution.py:537

commit v4 on v3

--- a/solution.py
+++ b/solution.py
@@ -22,7 +22,7 @@
 TOP = 128
 HB = 128
 LAGS = (0, 2, 4, 6, 8)
-DIRECT = 0
+DIRECT = 1
 SLOTS = 10
 CUTS = 2
 PIECE = BLOCK // CUTS
@@ -153,13 +153,14 @@
     pl.semaphore_wait(barrier, PEERS - 1 + 3)
 
     def start_parcel(k, carry):
-        to = (me + k) % PEERS
+        to = ((x + (k // 2) % NX) % NX) * 4 + ((yh + 1 + k // 8) % NY) * 2 + (c + k % 2) % NC
         remote(
             parcels.at[(to // 4) * 2 + to % 2], landed.at[me], a2a_s.at[0], a2a_r.at[0], peer(to)
         ).start()
         return carry
 
-    lax.fori_loop(1, PEERS, start_parcel, 0)
+    lax.fori_loop(0, PEERS // 2, start_parcel, 0)
+    lax.fori_loop(PEERS // 2 + 1, PEERS, start_parcel, 0)
     for copy in weight_sends(0):
         copy.start()
     parcels_whole = remote(
@@ -291,38 +292,27 @@
                 part[u, q, m * SHARE : (m + 1) * SHARE, :] = gates[rows, m * HB : (m + 1) * HB].astype(BF16)
             part[u, q, 4 * SHARE :, :] = (dhid[rows] * scale).astype(BF16)
 
-        @pl.when(ring(u))
-        def _():
-            x_start(
-                u,
-                SCATTER,
-                (F_LEFT, part.at[u, xo, top], via.at[u, top], right),
-                (F_RIGHT, part.at[u, xo, low], via.at[u, low], left),
-                (LEFT, part.at[u, xr, low], from_left.at[u, low], right),
-                (RIGHT, part.at[u, xl, top], from_right.at[u, top], left),
-            )
-
-        @pl.when(u >= units - DIRECT)
-        def _():
-            x_start(
-                u,
-                SCATTER,
-                (F_LEFT, part.at[u, xo], via.at[u], far),
-                (LEFT, part.at[u, xr], from_left.at[u], right),
-                (RIGHT, part.at[u, xl], from_right.at[u], left),
-            )
+        x_start(
+            u,
+            SCATTER,
+            (F_LEFT, part.at[u, xo, top], via.at[u, top], right),
+            (F_RIGHT, part.at[u, xo, low], via.at[u, low], left),
+            (LEFT, part.at[u, xr, low], from_left.at[u, low], right),
+            (RIGHT, part.at[u, xl, top], from_right.at[u, top], left),
+        )
 
     def mix(u):
-        @pl.when(ring(u))
-        def _():
-            x_wait(u, F_LEFT, via.at[u, top])
-            via[u, :TOP] = (via[u, :TOP].astype(F32) + part[u, xr, :TOP].astype(F32)).astype(BF16)
-            x_start(u, MIXED, (LEFT, via.at[u, top], from_left.at[u, top], right))
-            x_wait(u, F_RIGHT, via.at[u, low])
-            via[u, TOP:] = (via[u, TOP:].astype(F32) + part[u, xl, TOP:].astype(F32)).astype(BF16)
-            x_start(u, MIXED, (RIGHT, via.at[u, low], from_right.at[u, low], left))
-
-    def activate(u, stack):
+        x_wait(u, F_LEFT, via.at[u, top])
+        via[u, :TOP] = (via[u, :TOP].astype(F32) + part[u, xr, :TOP].astype(F32)).astype(BF16)
+        x_start(u, MIXED, (LEFT, via.at[u, top], from_left.at[u, top], right))
+        x_wait(u, F_RIGHT, via.at[u, low])
+        via[u, TOP:] = (via[u, TOP:].astype(F32) + part[u, xl, TOP:].astype(F32)).astype(BF16)
+        x_start(u, MIXED, (RIGHT, via.at[u, low], from_right.at[u, low], left))
+
+    def hidden(u):
+        x_wait(u, LEFT, from_left.at[u])
+        x_wait(u, RIGHT, from_right.at[u])
+        stack = part[u, x].astype(F32) + from_left[u].astype(F32) + from_right[u].astype(F32)
         gate, up, tgate, tup, dhid = (stack[m * SHARE : (m + 1) * SHARE] for m in range(5))
         sig = jax.nn.sigmoid(gate)
         first = sig * (1.0 + gate * (1.0 - sig))
@@ -336,19 +326,8 @@
             (T_RIGHT, tq.at[u, :, x], tq.at[u, :, x], left),
         )
 
-    def hidden(u):
-        x_wait(u, LEFT, from_left.at[u])
-        x_wait(u, RIGHT, from_right.at[u])
-
-        @pl.when(ring(u))
-        def _():
-            activate(u, part[u, x].astype(F32) + from_left[u].astype(F32) + from_right[u].astype(F32))
-
         @pl.when(u >= units - DIRECT)
         def _():
-            x_wait(u, F_LEFT, via.at[u])
-            near = part[u, x].astype(F32) + from_left[u].astype(F32)
-            activate(u, near + from_right[u].astype(F32) + via[u].astype(F32))
             x_start(u, TQ, (T_FAR, tq.at[u, :, x], tq.at[u, :, x], far))
 
     def pass_on(u):
@@ -412,16 +391,16 @@
                 for copy in out_copies(jj):
                     copy.start()
 
+        x_sent(u, SCATTER, part.at[u, pl.ds(0, 2)])
+        x_sent(u, MIXED, part.at[u, 0])
+
         @pl.when(ring(u))
         def _():
-            x_sent(u, SCATTER, part.at[u, pl.ds(0, 2)])
-            x_sent(u, MIXED, part.at[u, 0])
             x_sent(u, TQ, tq.at[u, :, pl.ds(0, 2)])
             x_sent(u, PASSED, tq.at[u, :, 0])
 
         @pl.when(u >= units - DIRECT)
         def _():
-            x_sent(u, SCATTER, part.at[u, pl.ds(0, 3)])
             x_sent(u, TQ, tq.at[u, :, pl.ds(0, 3)])
 
     def step(n, carry):

time: 104 us -> 104 us (level)
  no operation moved by 1% of the time
where the time goes in v4:
time: 104 us
  Pallas kernels  101 us (97%)
  other arithmetic  2.42 us (2%)
    pallas_call x1, Pallas kernels, per_device(): pl.pallas_call(functools.partial(kernel, blocks, scale), out_shape=(jax.S...  101 us
    add x1, other arithmetic, per_device(): return (own_gate + in_gate.astype(F32), own_up + in_up.astype(F32))  2.42 us

profile of v4, /device:TPU:2, one launch (start us, length us, event | category | flops | bytes accessed | tf_op | source)
XLA Modules:
  0.0 103.9 jit_solution(907750745722569347)
XLA Ops:
  0.6 100.9 %shard_map.86 = (f32[512,256]{1,0:T(8,128)}, f32[512,256]{1,0:T(8,128)}, bf16[512,256]{1,0:T(8,128)(2,1)}, bf16[512,256]{1,0:T(8,128)(2,1)}) custom-call(bf16[6,4096]{1,0:T(8,128)(2,1)} %tokens.1, bf16[512,256]{1,0:T(8,128)(2,1)} %w_gate.1, bf16[512,256]{1,0:T(8,128)(2,1)} %w_up.1, bf16[512,256]{1,0:T(8,128)(2,1)} %probe_gate.1, bf16[512,256]{1,0:T(8,128)(2,1)} %probe_up.1, ...), custom_call_target="tpu_custom_call" | custom-call | tf_op jit(solution)/shard_map/pallas_call | solution.py:476
  101.5 2.4 %convert_add_fusion = (f32[512,256]{1,0:T(8,128)}, f32[512,256]{1,0:T(8,128)}) fusion(f32[512,256]{1,0:T(8,128)} %get-tuple-element.8, bf16[512,256]{1,0:T(8,128)(2,1)} %get-tuple-element.9, f32[512,256]{1,0:T(8,128)} %get-tuple-element.6, bf16[512,256]{1,0:T(8,128)(2,1)} %get-tuple-element.7), kind=kLoop, calls=%fused_computation | loop fusion | flops 524288 | bytes 2621440 | tf_op jit(solution)/shard_map/add | solution.py:516
